TPU v7x, 32 devices: a whole 2x2x4 slice. The times are simulated.
32 devices in a mesh: grp: 4 (over y, x), tp: 8 (over z, core).
Axes of the slice: x: 2, y: 2, z: 4, core: 2. Of those that a mesh axis runs over, the one named last changes fastest.
Arguments:
- tokens: bfloat16 [384, 5120], P('grp'), may hold values from -36 to 36
- trainer_panels: bfloat16 [32, 5120, 128], P('tp', 'grp'), may hold values from -0.078125 to 0.078125
- panel_home: int32 [24], replicated, may hold values from 0 to 31, as said below
- lengths: int32 [4, 4], P('grp'), may hold values from 1 to 48, 96 in all within a row
Outputs:
- context: float32 [384, 1024], P(('grp', 'tp'))
Inputs may be any that keep to these rules, and one draw needn't show every extreme that they name: `panel_home`: entries are distinct; entry p is 4 times the tp index of the trainer device that holds panel p, plus the panel's slot on that device. Panels 0 to 7 are query heads, the next 8 key heads, the last 8 value heads. Some trainer device holds 4 panels.
All inputs are finite; a program needn't handle non-finite values.
Results may differ from a plain program's by a relative error of at most 0.012.
Values may be sent and summed in bfloat16 or wider, within the bound.
No kernel may reach another device: no remote copies, remote signals or barrier semaphores. Data moves between devices by JAX's collectives and lax.ppermute only.
A program may use at most 64 MiB of HBM per device.

v0:
```python
import jax
import jax.numpy as jnp
from jax import lax
from jax.sharding import PartitionSpec as P


def on_device(tokens, trainer_panels, panel_home, lengths):
    tp_count = lax.axis_size("tp")
    member_id = lax.axis_index("tp")
    kv_count = (panel_home.shape[0] - tp_count) // 2
    group_size = tp_count // kv_count
    slot_count = trainer_panels.shape[0]
    head_dim = trainer_panels.shape[2]
    needed = jnp.stack(
        [
            member_id,
            tp_count + member_id // group_size,
            tp_count + kv_count + member_id // group_size,
        ]
    )
    wanted = panel_home[needed]
    peer_ids = jnp.arange(tp_count, dtype=jnp.int32)
    reader_need = jnp.stack(
        [peer_ids, tp_count + peer_ids // group_size, tp_count + kv_count + peer_ids // group_size],
        axis=1,
    )
    reader_home = panel_home[reader_need]
    local_slot = reader_home - member_id * slot_count
    owned_here = (local_slot >= 0) & (local_slot < slot_count)
    picked = trainer_panels[jnp.clip(local_slot, 0, slot_count - 1)]
    outbound = jnp.where(owned_here[:, :, None, None], picked, jnp.zeros_like(picked))
    arrived = lax.all_to_all(outbound, "tp", split_axis=0, concat_axis=0, tiled=True)
    source = wanted // slot_count
    selected = jnp.stack([arrived[source[need_pos], need_pos] for need_pos in range(3)], axis=1)
    full_panels = lax.all_gather(selected, "grp", axis=0, tiled=True)
    weights = full_panels.reshape(full_panels.shape[0], 3 * head_dim)
    projected = jnp.dot(tokens, weights, preferred_element_type=jnp.float32).astype(jnp.bfloat16)
    query_rows = projected[:, :head_dim]
    key_rows = projected[:, head_dim : 2 * head_dim]
    value_rows = projected[:, 2 * head_dim :]
    seq_total = query_rows.shape[0]
    position = jnp.arange(seq_total, dtype=jnp.int32)
    bounds = jnp.cumsum(lengths[0])
    segment = jnp.sum((position[:, None] >= bounds[None, :]).astype(jnp.int32), axis=1)
    allowed = (segment[:, None] == segment[None, :]) & (position[None, :] <= position[:, None])
    score_scale = head_dim ** (-0.5)
    scores = (
        lax.dot_general(
            query_rows, key_rows, (((1,), (1,)), ((), ())), preferred_element_type=jnp.float32
        )
        * score_scale
    )
    masked = jnp.where(allowed, scores, -jnp.inf)
    row_peak = jnp.max(masked, axis=1, keepdims=True)
    row_exp = jnp.exp(masked - row_peak)
    attn_probs = (row_exp / jnp.sum(row_exp, axis=1, keepdims=True)).astype(jnp.bfloat16)
    context = jnp.dot(attn_probs, value_rows, preferred_element_type=jnp.float32)
    return lax.all_to_all(context, "tp", split_axis=0, concat_axis=1, tiled=True)


def solution(mesh):
    placed = (P("grp", None), P("tp", "grp", None), P(), P("grp", None))
    return jax.shard_map(
        on_device, mesh=mesh, in_specs=placed, out_specs=P(("grp", "tp"), None), check_vma=False
    )
```

profile of v0, /device:TPU:0, one launch (start us, length us, event | category | flops | bytes accessed | tf_op | source)
XLA Modules:
  0.0 284.0 jit_solution(13594505557828003359)
XLA Ops:
  6.5 0.0 copy-start
  6.6 0.1 copy.24
  6.6 0.1 reshape.278
  6.7 1.5 gather_fusion
  8.2 0.1 min.12
  8.3 0.1 copy.25
  8.4 0.1 copy.28
  8.5 0.1 reshape.286
  8.6 0.0 copy-done
  8.6 4.8 %gather_fusion.1 = bf16[24,1280,128]{2,1,0:T(8,128)(2,1)} fusion(bf16[4,1280,128]{2,1,0:T(8,128)(2,1)S(1)} %copy-done, s32[1024]{0:T(1024)S(1)} %pad_clamp_fusion.1), kind=kCustom, calls=%fused_computation.1 | custom fusion | bytes 15728736 | tf_op jit(solution)/shard_map/gather | solution.py:30
  13.3 10.6 %copy.29 = bf16[8,3,1280,128]{2,3,1,0:T(8,128)(2,1)} copy(bf16[8,3,1280,128]{3,2,1,0:T(8,128)(2,1)} %bitcast.34) | data formatting | bytes 15728640 | tf_op jit(solution)/shard_map/gather | solution.py:30
  23.9 0.1 reshape.312
  24.0 7.0 %broadcast_select_fusion = bf16[8,3,1280,128]{2,3,1,0:T(8,128)(2,1)} fusion(bf16[8,3,1280,128]{2,3,1,0:T(8,128)(2,1)} %copy.29, pred[8,3]{1,0:T(8,128)(4,1)S(1)} %reshape.312), kind=kLoop, calls=%fused_computation.3 | loop fusion | flops 3932160 | bytes 15728664 | tf_op jit(solution)/shard_map/jit(_where)/select_n | solution.py:31
  31.0 0.0 copy-start.1
  31.0 0.0 copy-start.3
  31.0 0.0 copy-start.2
  31.0 6.6 %all-to-all-start = ((bf16[8,3,1280,128]{2,3,1,0:T(8,128)(2,1)}), bf16[8,3,1280,128]{2,3,1,0:T(8,128)(2,1)}, u32[]{:S(2)}, u32[]{:S(2)}) async-start(bf16[8,3,1280,128]{2,3,1,0:T(8,128)(2,1)} %broadcast_select_fusion), calls=%async_computation | async-start | bytes 15728640 | tf_op jit(solution)/shard_map/all_to_all | solution.py:32
  37.6 0.0 all-gather.2.cloned.1.call-start
  37.7 0.1 fusion.9
  37.8 0.0 copy-done.1
  37.8 0.6 gather_fusion.2
  38.4 0.6 fusion.10
  44.5 165.9 %all-to-all-done = bf16[8,3,1280,128]{2,3,1,0:T(8,128)(2,1)} async-done(((bf16[8,3,1280,128]{2,3,1,0:T(8,128)(2,1)}), bf16[8,3,1280,128]{2,3,1,0:T(8,128)(2,1)}, u32[]{:S(2)}, u32[]{:S(2)}) %all-to-all-start) | async-done | bytes 7864352 | tf_op jit(solution)/shard_map/all_to_all | solution.py:32
  210.4 1.2 dynamic-slice_bitcast_fusion.2
  211.6 1.1 pad_maximum_fusion
  212.7 0.0 all-gather.2.cloned.1.call-update
  212.7 0.0 copy-done.3
  212.7 0.2 reduce-window.8
  212.9 0.1 convert_reduce_fusion
  213.0 49.3 %all-gather.2.cloned.1.call-done = bf16[5120,3,128]{0,2,1:T(8,128)(2,1)} async-done(((bf16[1280,3,128]{0,2,1:T(8,128)(2,1)}), bf16[5120,3,128]{0,2,1:T(8,128)(2,1)}) %all-gather.2.cloned.1.call-update) | async-done | bytes 3932176 | tf_op jit(solution)/shard_map/all_gather | solution.py:35
  262.3 0.0 copy-done.2
  262.3 3.4 %fusion = bf16[96,384]{1,0:T(8,128)(2,1)S(1)} fusion(bf16[5120,384]{0,1:T(8,128)(2,1)} %bitcast.35, bf16[96,5120]{1,0:T(8,128)(2,1)S(1)} %copy-done.2), kind=kOutput, calls=%fused_computation.5 | convolution fusion | flops 377524224 | bytes 4988928 | tf_op jit(solution)/shard_map/dot_general | solution.py:37
  265.7 0.2 fusion.11
  266.0 0.2 fusion.4
  266.2 10.3 %all_to_all.24 = f32[8,12,128]{2,1,0:T(8,128)S(1)} all-to-all(f32[8,12,128]{2,1,0:T(8,128)S(1)} %all_to_all.18), channel_id=1, replica_groups=mesh['grp'=4,'tp'=8] {'tp'}, dimensions={0} | all-to-all | bytes 98304 | tf_op jit(solution)/shard_map/all_to_all | solution.py:58
  276.5 0.6 copy.31
  (14 shorter events, 0.2 us)
Async XLA Ops:
  6.5 2.0 copy-start
  31.0 6.8 %copy-start.1 = (s32[24]{0:T(128)S(1)}, s32[24]{0:T(128)}, u32[]{:S(2)}) copy-start(s32[24]{0:T(128)} %param.6) | copy-start | bytes 292
  31.0 181.7 %copy-start.3 = (s32[1,4]{1,0:T(1,128)S(1)}, s32[1,4]{1,0:T(1,128)}, u32[]{:S(2)}) copy-start(s32[1,4]{1,0:T(1,128)} %param.7) | copy-start | bytes 52
  31.0 231.3 %copy-start.2 = (bf16[96,5120]{1,0:T(8,128)(2,1)S(1)}, bf16[96,5120]{1,0:T(8,128)(2,1)}, u32[]{:S(2)}) copy-start(bf16[96,5120]{1,0:T(8,128)(2,1)} %param.4) | copy-start | bytes 2949124
  31.0 179.4 %all-to-all-start = ((bf16[8,3,1280,128]{2,3,1,0:T(8,128)(2,1)}), bf16[8,3,1280,128]{2,3,1,0:T(8,128)(2,1)}, u32[]{:S(2)}, u32[]{:S(2)}) async-start(bf16[8,3,1280,128]{2,3,1,0:T(8,128)(2,1)} %broadcast_select_fusion), calls=%async_computation | async-start | bytes 15728640 | tf_op jit(solution)/shard_map/all_to_all | solution.py:32
  37.6 224.7 %all-gather.2.cloned.1.call-start = ((), (), s32[]{:S(2)}) async-start(), calls=%async_computation.2 | async-start | bytes 4915200 | tf_op jit(solution)/shard_map/all_gather | solution.py:35
Sparse Core Ops, SparseCore 0:
  212.8 49.4 all-gather.1
where the time goes:
time: 285 us; the launch traced here: 284 us
  waiting for transfers between devices  215 us (75%)
  local copies, waits for them, and re-layouts  20.6 us (7%)
  between operations  19 us (7%)
  blocking collectives  10.3 us (4%)
  other arithmetic  8.5 us (3%)
  starting transfers between devices  6.66 us (2%)
  matrix products  3.8 us (1%)
    all_to_all x1, waiting for transfers between devices, on_device(): lax.all_to_all(outbound, 'tp', split_axis=0, concat_axis=0, tiled=True)  166 us
    all_gather x1, waiting for transfers between devices, on_device(): full_panels = lax.all_gather(selected, 'grp', axis=0, tiled=True)  49.3 us
    gather x2, local copies, waits for them, and re-layouts, on_device(): picked = trainer_panels[jnp.clip(local_slot, 0, slot_count - 1)]  15.4 us
    all_to_all x1, blocking collectives, on_device(): lax.all_to_all(context, 'tp', split_axis=0, concat_axis=1, tiled=True)  10.3 us
    select_n x1, other arithmetic, on_device(): jnp.where(owned_here[:, :, None, None], picked, jnp.zeros_like(picked))  6.98 us
    all_to_all x1, starting transfers between devices, on_device(): lax.all_to_all(outbound, 'tp', split_axis=0, concat_axis=0, tiled=True)  6.62 us
  transfers between devices with their start and end apart: 2, of which 2 were waited for; matrix products, arithmetic and copies ran while one was open for 1% of the time, Pallas kernels for 0%

commit v1 on v0

v1 whole, which is shorter than its diff:
```python
import functools

import jax
import jax.numpy as jnp
from jax import lax
from jax.experimental import pallas as pl
from jax.experimental.pallas import tpu as pltpu
from jax.sharding import PartitionSpec as P

F32 = jnp.float32
BF16 = jnp.bfloat16
VMEM = pl.BlockSpec(memory_space=pltpu.VMEM)
SMEM = pl.BlockSpec(memory_space=pltpu.SMEM)
ROOM = 48 * 1024 * 1024


def split(turn, pairs, tokens, *refs):
    outs, (blocks, sems) = refs[-2 - len(pairs) : -2], refs[-2:]
    group, core = lax.axis_index("grp"), lax.rem(lax.axis_index("tp"), 2)
    depth = outs[0].shape[1]
    copies = []
    for at, pair in enumerate(pairs):
        column = pl.ds(pl.multiple_of((group ^ jnp.where(core == 0, *pair)) * depth, depth), depth)
        copies.append(pltpu.make_async_copy(tokens.at[:, column], blocks.at[at], sems.at[at]))
        copies[-1].start()
    for at, out in enumerate(outs):
        copies[at].wait()
        for which in (0, 1):

            @pl.when(core == which)
            def _():
                block = blocks[at].astype(F32)
                firsts = range(turn * which, block.shape[0], 2 * turn)
                picked = jnp.concatenate([block[first : first + turn] for first in firsts], axis=0)
                out[...] = picked.astype(out.dtype)


def project(groups, *refs):
    token_refs, (own, sibling), outs = refs[:groups], refs[groups : groups + 2], refs[groups + 2 :]
    core = lax.rem(lax.axis_index("tp"), 2)
    slots, _, width = own.shape
    rows = token_refs[0].shape[0]
    stacked = jnp.concatenate([token_ref[...] for token_ref in token_refs], axis=0)
    for place, panels in ((core, own), (1 - core, sibling)):
        many = 1 if groups == 1 else 2
        for slot in range(0, slots, many):
            pair = jnp.concatenate([panels[slot + i] for i in range(many)], axis=1)
            part = jnp.dot(stacked, pair, preferred_element_type=F32)
            column = pl.ds(pl.multiple_of((place * slots + slot) * width, many * width), many * width)
            for at, out in enumerate(outs):
                out[:, column] = part[at * rows : (at + 1) * rows].astype(out.dtype)


def total(chips, steps, *refs):
    outs, turns = refs[-1 - chips : -1], refs[-1]
    value = refs[0][...]
    for ref in refs[1 : -1 - chips]:
        value += ref[...].astype(F32)
    turn, columns = value.shape[0] // chips, value.shape[1]
    for at in range(chips):
        turns[at, :turn] = value[at * turn : (at + 1) * turn]
    chip = lax.axis_index("tp") // 2
    for step, out in zip(steps, outs):
        seen = out.shape[0] // 2 // turn
        picked = jnp.concatenate([turns[jnp.maximum((chip ^ step) - back, 0)][:turn] for back in range(seen)], axis=0)
        picked = jnp.concatenate([picked[:, : columns // 2], picked[:, columns // 2 :]], axis=0)
        out[...] = picked.astype(out.dtype)


def lay_out(chips, steps, pieces, held):
    chip = lax.axis_index("tp") // 2
    held_rows, columns = held.shape[1:]
    piece_rows = pieces[0].shape[0] // 2
    for step, piece in zip(steps, pieces):
        value = piece[...].astype(F32)
        rest = jnp.zeros((held_rows - piece_rows, columns // 2), F32)
        for side in (0, 1):
            part = value[side * piece_rows : (side + 1) * piece_rows]
            part = jnp.concatenate([part, rest], axis=0).astype(held.dtype)
            held[chip ^ step, :, side * (columns // 2) : (side + 1) * (columns // 2)] = part


def visible(half, rows, pad, held_rows, piece_rows, lengths):
    member = lax.axis_index("tp")
    local = lax.broadcasted_iota(jnp.int32, (1, held_rows), 1)
    back = sum((local >= turns * rows).astype(jnp.int32) for turns in range(1, piece_rows // rows))
    key_at = (member // 2) * (2 * rows) + half * rows + local - back * (3 * rows)
    key_at = jnp.where(local < piece_rows, key_at, -1)
    query_at = lax.broadcasted_iota(jnp.int32, (pad, 1), 0) + member * rows
    bound = jnp.zeros((1, 1), jnp.int32)
    since = jnp.zeros((pad, 1), jnp.int32)
    for response in range(lengths.shape[1]):
        since = jnp.where(query_at >= bound, bound, since)
        bound = bound + lengths[:, response : response + 1]
    return (key_at <= query_at) & (key_at >= since)


def reader(panel_home, held, width):
    homes = panel_home[...]
    places = lax.broadcasted_iota(jnp.int32, homes.shape, 1)
    per_chip = held.shape[2] // width

    def panel(index):
        slot = jnp.sum(jnp.where(places == index, homes, 0))
        at = pl.multiple_of(lax.rem(slot, per_chip) * width, width)
        return held.at[slot // per_chip, :, pl.ds(at, width)]

    return panel


def score(queries, panel, heads, kv_count, pad, allowed):
    scores = []
    for head in range(heads):
        key = panel(heads + head // (heads // kv_count))[...]
        query = queries[head * pad : (head + 1) * pad]
        part = lax.dot_general(query, key, (((1,), (1,)), ((), ())), preferred_element_type=F32)
        scores.append(jnp.where(allowed, part * key.shape[1] ** -0.5, -1e30))
    return jnp.concatenate(scores, axis=0)


def mix(weights, panel, heads, kv_count, pad):
    parts = []
    for head in range(heads):
        value = panel(heads + kv_count + head // (heads // kv_count))[...]
        parts.append(jnp.dot(weights[head * pad : (head + 1) * pad], value, preferred_element_type=F32))
    return jnp.concatenate(parts, axis=0)


def attend_own(chips, steps, rows, heads, panel_home, lengths, *refs):
    pieces, (queries, peak, mass, mixed, held) = refs[:chips], refs[chips:]
    lay_out(chips, steps, pieces, held)
    width = queries.shape[1]
    kv_count = (panel_home.shape[1] - heads) // 2
    pad = queries.shape[0] // heads
    half = lax.rem(lax.axis_index("tp"), 2)
    allowed = visible(half, rows, pad, held.shape[1], pieces[0].shape[0] // 2, lengths)
    panel = reader(panel_home, held, width)
    query = jnp.concatenate([panel(head)[:pad] for head in range(heads)], axis=0)
    queries[...] = query
    scores = score(query, panel, heads, kv_count, pad, allowed)
    top = jnp.max(scores, axis=1, keepdims=True)
    weights = jnp.exp(scores - top)
    peak[...] = jnp.broadcast_to(top, peak.shape)
    mass[...] = jnp.broadcast_to(jnp.sum(weights, axis=1, keepdims=True), mass.shape)
    mixed[...] = mix(weights.astype(BF16), panel, heads, kv_count, pad)


def attend_rest(chips, steps, panel_home, lengths, queries, peak, mass, mixed, *refs):
    pieces, (out, held) = refs[:chips], refs[chips:]
    lay_out(chips, steps, pieces, held)
    rows, width = out.shape[0], queries.shape[1]
    heads = out.shape[1] // width
    kv_count = (panel_home.shape[1] - heads) // 2
    pad = queries.shape[0] // heads
    half = 1 - lax.rem(lax.axis_index("tp"), 2)
    allowed = visible(half, rows, pad, held.shape[1], pieces[0].shape[0] // 2, lengths)
    panel = reader(panel_home, held, width)
    scores = score(queries[...], panel, heads, kv_count, pad, allowed)
    before = peak[:, :1]
    top = jnp.maximum(before, jnp.max(scores, axis=1, keepdims=True))
    weights = jnp.exp(scores - top)
    kept = jnp.exp(before - top)
    whole = mass[:, :1] * kept + jnp.sum(weights, axis=1, keepdims=True)
    value = mixed[...] * kept + mix(weights.astype(BF16), panel, heads, kv_count, pad)
    value = value / whole
    for head in range(heads):
        out[:, head * width : (head + 1) * width] = value[head * pad : head * pad + rows]


def call(body, outs, in_specs, out_specs, scratch=(), flops=0, nbytes=0):
    return pl.pallas_call(
        body,
        out_shape=outs,
        in_specs=in_specs,
        out_specs=out_specs,
        scratch_shapes=scratch,
        compiler_params=pltpu.CompilerParams(vmem_limit_bytes=ROOM),
        cost_estimate=pl.CostEstimate(flops=flops, bytes_accessed=nbytes, transcendentals=0),
    )


def swap(x, axis, distance):
    size = lax.axis_size(axis)
    return lax.ppermute(x, axis, [(i, i ^ distance) for i in range(size)])


def swap_groups(x, pair):
    groups, members = lax.axis_size("grp"), lax.axis_size("tp")
    places = [(g * members + t, (g ^ pair[t % 2]) * members + t) for g in range(groups) for t in range(members)]
    return lax.ppermute(x, ("grp", "tp"), places)


def on_device(tokens, trainer_panels, panel_home, lengths):
    groups, members = lax.axis_size("grp"), lax.axis_size("tp")
    group, core = lax.axis_index("grp"), lax.rem(lax.axis_index("tp"), 2)
    chips = members // 2
    slots, depth, width = trainer_panels.shape
    rows, model = tokens.shape
    half, turn = rows // 2, rows // members
    columns = 2 * slots * width

    sibling = swap(trainer_panels, "tp", 1)
    pairs = [(0, 0), *zip(range(1, groups - 1), range(groups - 2, 0, -1)), (groups - 1, groups - 1)]
    if depth % 128 == 0:
        in_hbm = pltpu.with_memory_space_constraint(tokens, pltpu.HBM)

        def cut(pairs, *before):
            return list(
                call(
                    functools.partial(split, turn, pairs),
                    [jax.ShapeDtypeStruct((half, depth), BF16)] * len(pairs),
                    [pl.BlockSpec(memory_space=pltpu.HBM)] + [pl.BlockSpec(memory_space=pl.ANY)] * len(before),
                    [VMEM] * len(pairs),
                    scratch=[pltpu.VMEM((len(pairs), rows, depth), BF16), pltpu.SemaphoreType.DMA((len(pairs),))],
                    nbytes=2 * len(pairs) * rows * depth,
                )(in_hbm, *before)
            )

        far = cut(pairs[-1:])
        near = cut(pairs[1:-1], far[0])
        blocks = cut(pairs[:1], near[0]) + near + far
    else:
        turns = tokens.reshape(chips, 2, turn, model)
        blocks = [
            lax.dynamic_slice(
                turns, (0, core, 0, (group ^ jnp.where(core == 0, *pair)) * depth), (chips, 1, turn, depth)
            ).reshape(half, depth)
            for pair in pairs
        ]
    batches = [groups - 1], list(range(1, groups - 1))
    arrived = {step: swap_groups(blocks[step], pairs[step]) for steps in batches for step in steps}

    def products(token_blocks, dtype):
        return call(
            functools.partial(project, len(token_blocks)),
            [jax.ShapeDtypeStruct((half, columns), dtype)] * len(token_blocks),
            [VMEM] * (len(token_blocks) + 2),
            [VMEM] * len(token_blocks),
            flops=2 * len(token_blocks) * half * depth * columns,
            nbytes=2 * depth * columns,
        )(*token_blocks, trainer_panels, sibling)

    kept = products(blocks[:1], F32)
    parts = []
    for steps in batches:
        batch = [arrived[step] for step in steps]
        if not parts:
            kept, batch = lax.optimization_barrier((kept, batch))
        sent = products(batch, BF16)
        parts += [swap_groups(part, pairs[step]) for step, part in zip(steps, sent)]

    seen = min(chips, -(-(half - 1) // (2 * turn)) + 1)
    steps = list(range(chips // 2, chips)) + list(range(chips // 2 - 1, -1, -1))
    pieces = call(
        functools.partial(total, chips, steps),
        [jax.ShapeDtypeStruct((2 * seen * turn, columns // 2), BF16)] * chips,
        [VMEM] * groups,
        [VMEM] * chips,
        scratch=[pltpu.VMEM((chips, -(-turn // 8) * 8, columns), F32)],
        nbytes=2 * groups * half * columns,
    )(*kept, parts[0], *parts[:0:-1])
    pieces = [swap(piece, "tp", 2 * step) if step else piece for step, piece in zip(steps, pieces)]
    others = [swap(piece, "tp", 1) for piece in pieces[::-1]][::-1]
    held = pltpu.VMEM((chips, -(-seen * turn // 16) * 16, columns), BF16)
    homes = panel_home.reshape(1, -1)
    queries = members * -(-turn // 16) * 16
    so_far = call(
        functools.partial(attend_own, chips, steps, turn, members),
        [jax.ShapeDtypeStruct((queries, width), BF16)] + [jax.ShapeDtypeStruct((queries, width), F32)] * 3,
        [VMEM] * (2 + chips),
        [VMEM] * 4,
        scratch=[held],
        nbytes=2 * chips * half * columns,
    )(homes, lengths, *pieces)
    return call(
        functools.partial(attend_rest, chips, steps),
        jax.ShapeDtypeStruct((turn, members * width), F32),
        [VMEM] * (6 + chips),
        VMEM,
        scratch=[held],
        nbytes=2 * chips * half * columns,
    )(homes, lengths, *so_far, *others)


def solution(mesh):
    placed = (P("grp", None), P("tp", "grp", None), P(), P("grp", None))
    return jax.shard_map(
        on_device, mesh=mesh, in_specs=placed, out_specs=P(("grp", "tp"), None), check_vma=False
    )
```

time: 285 us -> 30.5 us (0.11)
  waiting for transfers between devices: 215 us -> 9.04 us
  local copies, waits for them, and re-layouts: 20.6 us -> 0.02 us
  between operations: 19 us -> 0.12 us
  blocking collectives: 10.3 us -> 0 us
  other arithmetic: 8.5 us -> 0 us
  starting transfers between devices: 6.66 us -> 14.6 us
  Pallas kernels: 0 us -> 6.58 us
  matrix products: 3.8 us -> 0 us
    all_to_all x1 -> x0, waiting for transfers between devices: 166 us -> none  [on_device(): lax.all_to_all(outbound, 'tp', split_axis=0, concat_axis=0, tiled=True)]
    all_gather x1 -> x0, waiting for transfers between devices: 49.3 us -> none  [on_device(): full_panels = lax.all_gather(selected, 'grp', axis=0, tiled=True)]
    gather x4 -> x0, local copies, waits for them, and re-layouts: 17.5 us -> none  [the longest x2 15.4 us: on_device(): picked = trainer_panels[jnp.clip(local_slot, 0, slot_count - 1)]]
    ppermute x0 -> x14, starting transfers between devices: none -> 14.6 us  [the longest x6 9.55 us: swap_groups(): return lax.ppermute(x, ('grp', 'tp'), places)]
    all_to_all x1 -> x0, blocking collectives: 10.3 us -> none  [on_device(): lax.all_to_all(context, 'tp', split_axis=0, concat_axis=1, tiled=True)]
    ppermute x0 -> x14, waiting for transfers between devices: none -> 9.04 us  [the longest x8 5.23 us: swap(): return lax.ppermute(x, axis, [(i, i ^ distance) for i in range(size)])]
    select_n x5 -> x0, other arithmetic: 7.09 us -> none  [the longest x1 6.98 us: on_device(): jnp.where(owned_here[:, :, None, None], picked, jnp.zeros_like(picked))]
    all_to_all x1 -> x0, starting transfers between devices: 6.62 us -> none  [on_device(): lax.all_to_all(outbound, 'tp', split_axis=0, concat_axis=0, tiled=True)]
  transfers between devices with their start and end apart: 2 -> 14, of which waited for: 2 -> 8; matrix products, arithmetic and copies ran while one was open for 1% -> 0% of each run, Pallas kernels for 0% -> 17%
where the time goes in v1:
time: 30.5 us; the launch traced here: 30.3 us
  starting transfers between devices  14.6 us (48%)
  waiting for transfers between devices  9.04 us (30%)
  Pallas kernels  6.58 us (22%)
    ppermute x6, starting transfers between devices, swap_groups(): return lax.ppermute(x, ('grp', 'tp'), places)  9.55 us
    ppermute x8, waiting for transfers between devices, swap(): return lax.ppermute(x, axis, [(i, i ^ distance) for i in range(size)])  5.23 us
    ppermute x8, starting transfers between devices, swap(): return lax.ppermute(x, axis, [(i, i ^ distance) for i in range(size)])  5.03 us
    ppermute x6, waiting for transfers between devices, swap_groups(): return lax.ppermute(x, ('grp', 'tp'), places)  3.81 us
    pallas_call x3, Pallas kernels, cut(): call(functools.partial(split, turn, pairs), [jax.ShapeDtypeStruct((half,...  3.06 us
    pallas_call x3, Pallas kernels, products(): call(functools.partial(project, len(token_blocks)), [jax.ShapeDtypeStruct...  1.56 us
    pallas_call x1, Pallas kernels, on_device(): call(functools.partial(attend_rest, chips, steps), jax.ShapeDtypeStruct((...  1.26 us
  transfers between devices with their start and end apart: 14, of which 8 were waited for; matrix products, arithmetic and copies ran while one was open for 0% of the time, Pallas kernels for 17%

profile of v1, /device:TPU:0, one launch (start us, length us, event | category | flops | bytes accessed | tf_op | source)
XLA Modules:
  0.0 30.3 jit_solution(12691590329515171316)
XLA Ops:
  0.0 0.5 %collective-permute-start = (bf16[4,1280,128]{2,1,0:T(8,128)(2,1)}, bf16[4,1280,128]{2,1,0:T(8,128)(2,1)S(1)}, u32[]{:S(2)}, u32[]{:S(2)}) collective-permute-start(bf16[4,1280,128]{2,1,0:T(8,128)(2,1)} %refs_2_.1), channel_id=1, source_target_pairs={{0,1},{1,0},{2,3},{3,2},{4,5},{5,4},{6,7},{7,6},{8,9},{9,8},{10,11... | collective-permute-start | bytes 3932168 | tf_op jit(solution)/shard_map/ppermute | solution.py:184
  0.5 1.0 %shard_map.46.refs_0_ = bf16[48,1280]{1,0:T(8,128)(2,1)S(1)} custom-call(bf16[96,5120]{1,0:T(8,128)(2,1)} %tokens.5), custom_call_target="tpu_custom_call" | custom-call | bytes 245760 | tf_op jit(solution)/shard_map/pallas_call | solution.py:209
  1.4 0.0 copy-start
  1.5 3.5 %collective-permute-start.1 = (bf16[48,1280]{1,0:T(8,128)(2,1)S(1)}, bf16[48,1280]{1,0:T(8,128)(2,1)S(1)}, u32[]{:S(2)}, u32[]{:S(2)}) collective-permute-start(bf16[48,1280]{1,0:T(8,128)(2,1)S(1)} %shard_map.46.refs_0_), channel_id=1, source_target_pairs={{0,24},{1,25},{2,26},{3,27},{4,28},{5,29},{6,30},{7,31},{8,16},{9,... | collective-permute-start | bytes 368648 | tf_op jit(solution)/shard_map/ppermute | solution.py:190
  5.0 1.1 %shard_map.47 = (bf16[48,1280]{1,0:T(8,128)(2,1)S(1)}, bf16[48,1280]{1,0:T(8,128)(2,1)S(1)}) custom-call(bf16[96,5120]{1,0:T(8,128)(2,1)} %tokens.5, bf16[48,1280]{1,0:T(8,128)(2,1)S(1)} %shard_map.46.refs_0_), custom_call_target="tpu_custom_call" | custom-call | bytes 491520 | tf_op jit(solution)/shard_map/pallas_call | solution.py:209
  6.1 0.6 %collective-permute-start.4 = (bf16[48,1280]{1,0:T(8,128)(2,1)S(1)}, bf16[48,1280]{1,0:T(8,128)(2,1)S(1)}, u32[]{:S(2)}, u32[]{:S(2)}) collective-permute-start(bf16[48,1280]{1,0:T(8,128)(2,1)S(1)} %get-tuple-element.22), channel_id=1, source_target_pairs={{0,16},{1,9},{2,18},{3,11},{4,20},{5,13},{6,22},{7,15},{8,24},{9,1... | collective-permute-start | bytes 368648 | tf_op jit(solution)/shard_map/ppermute | solution.py:190
  6.6 0.2 collective-permute-start.3
  6.8 1.0 %shard_map.48.refs_0_ = bf16[48,1280]{1,0:T(8,128)(2,1)S(1)} custom-call(bf16[96,5120]{1,0:T(8,128)(2,1)} %tokens.5, bf16[48,1280]{1,0:T(8,128)(2,1)S(1)} %get-tuple-element.19.refs_0_), custom_call_target="tpu_custom_call" | custom-call | bytes 245760 | tf_op jit(solution)/shard_map/pallas_call | solution.py:209
  7.8 0.0 collective-permute-done.refs_2_.refs_3_
  7.8 0.0 copy-done
  7.8 0.5 %shard_map.49.refs_0_ = f32[48,1024]{1,0:T(8,128)S(1)} custom-call(bf16[48,1280]{1,0:T(8,128)(2,1)S(1)} %shard_map.48.refs_0_, bf16[4,1280,128]{2,1,0:T(8,128)(2,1)S(1)} %copy-done, bf16[4,1280,128]{2,1,0:T(8,128)(2,1)S(1)} %collective-permute-done.refs_2_.refs_3_), custom_call_target="tpu_custom_call" | custom-call | flops 125829120 | bytes 2621440 | tf_op jit(solution)/shard_map/pallas_call | solution.py:234
  8.4 0.6 %collective-permute-done.1.refs_0_ = bf16[48,1280]{1,0:T(8,128)(2,1)S(1)} collective-permute-done((bf16[48,1280]{1,0:T(8,128)(2,1)S(1)}, bf16[48,1280]{1,0:T(8,128)(2,1)S(1)}, u32[]{:S(2)}, u32[]{:S(2)}) %collective-permute-start.1) | collective-permute-done | bytes 122912 | tf_op jit(solution)/shard_map/ppermute | solution.py:190
  9.0 0.5 %shard_map.50 = bf16[48,1024]{1,0:T(8,128)(2,1)S(1)} custom-call(bf16[48,1280]{1,0:T(8,128)(2,1)S(1)} %collective-permute-done.1.refs_0_, bf16[4,1280,128]{2,1,0:T(8,128)(2,1)S(1)} %copy-done, bf16[4,1280,128]{2,1,0:T(8,128)(2,1)S(1)} %collective-permute-done.refs_2_.refs_3_), custom_call_target="tpu_custom_call" | custom-call | flops 125829120 | bytes 2621440 | tf_op jit(solution)/shard_map/pallas_call | solution.py:234
  9.4 0.0 copy-start.1
  9.5 0.0 copy-start.2
  9.5 3.1 %collective-permute-start.2 = (bf16[48,1024]{1,0:T(8,128)(2,1)S(1)}, bf16[48,1024]{1,0:T(8,128)(2,1)S(1)}, u32[]{:S(2)}, u32[]{:S(2)}) collective-permute-start(bf16[48,1024]{1,0:T(8,128)(2,1)S(1)} %shard_map.50), channel_id=1, source_target_pairs={{0,24},{1,25},{2,26},{3,27},{4,28},{5,29},{6,30},{7,31},{8,16},{9,... | collective-permute-start | bytes 294920 | tf_op jit(solution)/shard_map/ppermute | solution.py:190
  12.6 0.0 collective-permute-done.4.refs_1_
  12.6 0.0 collective-permute-done.3.refs_0_
  12.6 0.6 %shard_map.51 = (bf16[48,1024]{1,0:T(8,128)(2,1)S(1)}, bf16[48,1024]{1,0:T(8,128)(2,1)S(1)}) custom-call(bf16[48,1280]{1,0:T(8,128)(2,1)S(1)} %collective-permute-done.3.refs_0_, bf16[48,1280]{1,0:T(8,128)(2,1)S(1)} %collective-permute-done.4.refs_1_, bf16[4,1280,128]{2,1,0:T(8,128)(2,1)S(1)} %copy-done, ...), custom_call_target="tpu_custom_call" | custom-call | flops 251658240 | bytes 2621440 | tf_op jit(solution)/shard_map/pallas_call | solution.py:234
  13.1 0.8 %collective-permute-start.5 = (bf16[48,1024]{1,0:T(8,128)(2,1)S(1)}, bf16[48,1024]{1,0:T(8,128)(2,1)S(1)}, u32[]{:S(2)}, u32[]{:S(2)}) collective-permute-start(bf16[48,1024]{1,0:T(8,128)(2,1)S(1)} %get-tuple-element.23), channel_id=1, source_target_pairs={{0,16},{1,9},{2,18},{3,11},{4,20},{5,13},{6,22},{7,15},{8,24},{9,1... | collective-permute-start | bytes 294920 | tf_op jit(solution)/shard_map/ppermute | solution.py:190
  13.9 1.4 %collective-permute-start.6 = (bf16[48,1024]{1,0:T(8,128)(2,1)S(1)}, bf16[48,1024]{1,0:T(8,128)(2,1)S(1)}, u32[]{:S(2)}, u32[]{:S(2)}) collective-permute-start(bf16[48,1024]{1,0:T(8,128)(2,1)S(1)} %get-tuple-element.24), channel_id=1, source_target_pairs={{0,8},{1,17},{2,10},{3,19},{4,12},{5,21},{6,14},{7,23},{8,0},{9,25... | collective-permute-start | bytes 294920 | tf_op jit(solution)/shard_map/ppermute | solution.py:190
  15.3 0.0 collective-permute-done.2.refs_1_
  15.4 3.1 %collective-permute-done.5.refs_2_ = bf16[48,1024]{1,0:T(8,128)(2,1)S(1)} collective-permute-done((bf16[48,1024]{1,0:T(8,128)(2,1)S(1)}, bf16[48,1024]{1,0:T(8,128)(2,1)S(1)}, u32[]{:S(2)}, u32[]{:S(2)}) %collective-permute-start.5) | collective-permute-done | bytes 98336 | tf_op jit(solution)/shard_map/ppermute | solution.py:190
  18.4 0.1 collective-permute-done.6.refs_3_
  18.5 0.1 shard_map.52
  18.7 2.7 %collective-permute-start.7 = (bf16[72,512]{1,0:T(8,128)(2,1)S(1)}, bf16[72,512]{1,0:T(8,128)(2,1)S(1)}, u32[]{:S(2)}, u32[]{:S(2)}) collective-permute-start(bf16[72,512]{1,0:T(8,128)(2,1)S(1)} %get-tuple-element.25), channel_id=1, source_target_pairs={{0,4},{1,5},{2,6},{3,7},{4,0},{5,1},{6,2},{7,3},{8,12},{9,13},{10,... | collective-permute-start | bytes 221192 | tf_op jit(solution)/shard_map/ppermute | solution.py:184
  21.3 1.3 %collective-permute-start.8 = (bf16[72,512]{1,0:T(8,128)(2,1)S(1)}, bf16[72,512]{1,0:T(8,128)(2,1)S(1)}, u32[]{:S(2)}, u32[]{:S(2)}) collective-permute-start(bf16[72,512]{1,0:T(8,128)(2,1)S(1)} %get-tuple-element.26), channel_id=1, source_target_pairs={{0,6},{1,7},{2,4},{3,5},{4,2},{5,3},{6,0},{7,1},{8,14},{9,15},{10,... | collective-permute-start | bytes 221192 | tf_op jit(solution)/shard_map/ppermute | solution.py:184
  22.7 0.2 collective-permute-start.9
  22.9 0.0 collective-permute-start.13
  22.9 3.3 %collective-permute-done.7.refs_0_ = bf16[72,512]{1,0:T(8,128)(2,1)S(1)} collective-permute-done((bf16[72,512]{1,0:T(8,128)(2,1)S(1)}, bf16[72,512]{1,0:T(8,128)(2,1)S(1)}, u32[]{:S(2)}, u32[]{:S(2)}) %collective-permute-start.7) | collective-permute-done | bytes 73760 | tf_op jit(solution)/shard_map/ppermute | solution.py:184
  26.2 0.0 collective-permute-start.10
  26.2 1.4 %collective-permute-done.8.refs_1_ = bf16[72,512]{1,0:T(8,128)(2,1)S(1)} collective-permute-done((bf16[72,512]{1,0:T(8,128)(2,1)S(1)}, bf16[72,512]{1,0:T(8,128)(2,1)S(1)}, u32[]{:S(2)}, u32[]{:S(2)}) %collective-permute-start.8) | collective-permute-done | bytes 73760 | tf_op jit(solution)/shard_map/ppermute | solution.py:184
  27.6 0.0 collective-permute-start.11
  27.6 0.2 collective-permute-done.9.refs_2_
  27.8 0.3 %collective-permute-start.12 = (bf16[72,512]{1,0:T(8,128)(2,1)S(1)}, bf16[72,512]{1,0:T(8,128)(2,1)S(1)}, u32[]{:S(2)}, u32[]{:S(2)}) collective-permute-start(bf16[72,512]{1,0:T(8,128)(2,1)S(1)} %collective-permute-done.9.refs_2_), channel_id=1, source_target_pairs={{0,1},{1,0},{2,3},{3,2},{4,5},{5,4},{6,7},{7,6},{8,9},{9,8},{10,11... | collective-permute-start | bytes 221192 | tf_op jit(solution)/shard_map/ppermute | solution.py:184
  28.1 0.0 copy-done.1
  28.1 0.0 copy-done.2
  28.1 0.6 %shard_map.53 = (bf16[128,128]{1,0:T(8,128)(2,1)S(1)}, f32[128,128]{1,0:T(8,128)S(1)}, f32[128,128]{1,0:T(8,128)S(1)}, f32[128,128]{1,0:T(8,128)S(1)}) custom-call(s32[1,24]{1,0:T(1,128)S(1)} %bitcast.1, s32[1,4]{1,0:T(1,128)S(1)} %copy-done.2, bf16[72,512]{1,0:T(8,128)(2,1)S(1)} %collective-permute-done.7.refs_0_, ...), custom_call_target="tpu_custom_call" | custom-call | bytes 393216 | tf_op jit(solution)/shard_map/pallas_call | solution.py:267
  28.7 0.0 collective-permute-done.13.refs_3_
  28.7 0.0 collective-permute-done.10.refs_0_
  28.8 0.1 collective-permute-done.11.refs_1_
  28.9 0.2 collective-permute-done.12.refs_2_
  29.1 1.3 %shard_map.54 = f32[12,1024]{1,0:T(8,128)} custom-call(s32[1,24]{1,0:T(1,128)S(1)} %bitcast.2, s32[1,4]{1,0:T(1,128)S(1)} %copy-done.2, bf16[128,128]{1,0:T(8,128)(2,1)S(1)} %get-tuple-element.29.queries, f32[128,128]{1,0:T(8,128)S(1)} %get-tuple-element.30.peak, f32[128,128]{1,0:T(8,128)S(1)} %get-tuple-element.31.mass, ...), custom_call_target="tpu_custom_call" | custom-call | bytes 393216 | tf_op jit(solution)/shard_map/pallas_call | solution.py:275
Async XLA Ops:
  0.0 7.8 %collective-permute-start = (bf16[4,1280,128]{2,1,0:T(8,128)(2,1)}, bf16[4,1280,128]{2,1,0:T(8,128)(2,1)S(1)}, u32[]{:S(2)}, u32[]{:S(2)}) collective-permute-start(bf16[4,1280,128]{2,1,0:T(8,128)(2,1)} %refs_2_.1), channel_id=1, source_target_pairs={{0,1},{1,0},{2,3},{3,2},{4,5},{5,4},{6,7},{7,6},{8,9},{9,8},{10,11... | collective-permute-start | bytes 3932168 | tf_op jit(solution)/shard_map/ppermute | solution.py:184
  1.4 6.4 %copy-start = (bf16[4,1280,128]{2,1,0:T(8,128)(2,1)S(1)}, bf16[4,1280,128]{2,1,0:T(8,128)(2,1)}, u32[]{:S(2)}) copy-start(bf16[4,1280,128]{2,1,0:T(8,128)(2,1)} %refs_2_.1) | copy-start | bytes 3932164
  1.5 7.5 %collective-permute-start.1 = (bf16[48,1280]{1,0:T(8,128)(2,1)S(1)}, bf16[48,1280]{1,0:T(8,128)(2,1)S(1)}, u32[]{:S(2)}, u32[]{:S(2)}) collective-permute-start(bf16[48,1280]{1,0:T(8,128)(2,1)S(1)} %shard_map.46.refs_0_), channel_id=1, source_target_pairs={{0,24},{1,25},{2,26},{3,27},{4,28},{5,29},{6,30},{7,31},{8,16},{9,... | collective-permute-start | bytes 368648 | tf_op jit(solution)/shard_map/ppermute | solution.py:190
  6.1 6.5 %collective-permute-start.4 = (bf16[48,1280]{1,0:T(8,128)(2,1)S(1)}, bf16[48,1280]{1,0:T(8,128)(2,1)S(1)}, u32[]{:S(2)}, u32[]{:S(2)}) collective-permute-start(bf16[48,1280]{1,0:T(8,128)(2,1)S(1)} %get-tuple-element.22), channel_id=1, source_target_pairs={{0,16},{1,9},{2,18},{3,11},{4,20},{5,13},{6,22},{7,15},{8,24},{9,1... | collective-permute-start | bytes 368648 | tf_op jit(solution)/shard_map/ppermute | solution.py:190
  6.6 5.9 %collective-permute-start.3 = (bf16[48,1280]{1,0:T(8,128)(2,1)S(1)}, bf16[48,1280]{1,0:T(8,128)(2,1)S(1)}, u32[]{:S(2)}, u32[]{:S(2)}) collective-permute-start(bf16[48,1280]{1,0:T(8,128)(2,1)S(1)} %get-tuple-element.19.refs_0_), channel_id=1, source_target_pairs={{0,8},{1,17},{2,10},{3,19},{4,12},{5,21},{6,14},{7,23},{8,0},{9,25... | collective-permute-start | bytes 368648 | tf_op jit(solution)/shard_map/ppermute | solution.py:190
  9.4 18.7 %copy-start.1 = (s32[24]{0:T(128)S(1)}, s32[24]{0:T(128)}, u32[]{:S(2)}) copy-start(s32[24]{0:T(128)} %param.6) | copy-start | bytes 292
  9.5 18.7 %copy-start.2 = (s32[1,4]{1,0:T(1,128)S(1)}, s32[1,4]{1,0:T(1,128)}, u32[]{:S(2)}) copy-start(s32[1,4]{1,0:T(1,128)} %lengths.3) | copy-start | bytes 52
  9.5 5.9 %collective-permute-start.2 = (bf16[48,1024]{1,0:T(8,128)(2,1)S(1)}, bf16[48,1024]{1,0:T(8,128)(2,1)S(1)}, u32[]{:S(2)}, u32[]{:S(2)}) collective-permute-start(bf16[48,1024]{1,0:T(8,128)(2,1)S(1)} %shard_map.50), channel_id=1, source_target_pairs={{0,24},{1,25},{2,26},{3,27},{4,28},{5,29},{6,30},{7,31},{8,16},{9,... | collective-permute-start | bytes 294920 | tf_op jit(solution)/shard_map/ppermute | solution.py:190
  13.1 5.3 %collective-permute-start.5 = (bf16[48,1024]{1,0:T(8,128)(2,1)S(1)}, bf16[48,1024]{1,0:T(8,128)(2,1)S(1)}, u32[]{:S(2)}, u32[]{:S(2)}) collective-permute-start(bf16[48,1024]{1,0:T(8,128)(2,1)S(1)} %get-tuple-element.23), channel_id=1, source_target_pairs={{0,16},{1,9},{2,18},{3,11},{4,20},{5,13},{6,22},{7,15},{8,24},{9,1... | collective-permute-start | bytes 294920 | tf_op jit(solution)/shard_map/ppermute | solution.py:190
  13.9 4.6 %collective-permute-start.6 = (bf16[48,1024]{1,0:T(8,128)(2,1)S(1)}, bf16[48,1024]{1,0:T(8,128)(2,1)S(1)}, u32[]{:S(2)}, u32[]{:S(2)}) collective-permute-start(bf16[48,1024]{1,0:T(8,128)(2,1)S(1)} %get-tuple-element.24), channel_id=1, source_target_pairs={{0,8},{1,17},{2,10},{3,19},{4,12},{5,21},{6,14},{7,23},{8,0},{9,25... | collective-permute-start | bytes 294920 | tf_op jit(solution)/shard_map/ppermute | solution.py:190
  18.7 7.5 %collective-permute-start.7 = (bf16[72,512]{1,0:T(8,128)(2,1)S(1)}, bf16[72,512]{1,0:T(8,128)(2,1)S(1)}, u32[]{:S(2)}, u32[]{:S(2)}) collective-permute-start(bf16[72,512]{1,0:T(8,128)(2,1)S(1)} %get-tuple-element.25), channel_id=1, source_target_pairs={{0,4},{1,5},{2,6},{3,7},{4,0},{5,1},{6,2},{7,3},{8,12},{9,13},{10,... | collective-permute-start | bytes 221192 | tf_op jit(solution)/shard_map/ppermute | solution.py:184
  21.3 6.3 %collective-permute-start.8 = (bf16[72,512]{1,0:T(8,128)(2,1)S(1)}, bf16[72,512]{1,0:T(8,128)(2,1)S(1)}, u32[]{:S(2)}, u32[]{:S(2)}) collective-permute-start(bf16[72,512]{1,0:T(8,128)(2,1)S(1)} %get-tuple-element.26), channel_id=1, source_target_pairs={{0,6},{1,7},{2,4},{3,5},{4,2},{5,3},{6,0},{7,1},{8,14},{9,15},{10,... | collective-permute-start | bytes 221192 | tf_op jit(solution)/shard_map/ppermute | solution.py:184
  22.7 5.1 %collective-permute-start.9 = (bf16[72,512]{1,0:T(8,128)(2,1)S(1)}, bf16[72,512]{1,0:T(8,128)(2,1)S(1)}, u32[]{:S(2)}, u32[]{:S(2)}) collective-permute-start(bf16[72,512]{1,0:T(8,128)(2,1)S(1)} %get-tuple-element.27), channel_id=1, source_target_pairs={{0,2},{1,3},{2,0},{3,1},{4,6},{5,7},{6,4},{7,5},{8,10},{9,11},{10,... | collective-permute-start | bytes 221192 | tf_op jit(solution)/shard_map/ppermute | solution.py:184
  22.9 5.8 %collective-permute-start.13 = (bf16[72,512]{1,0:T(8,128)(2,1)S(1)}, bf16[72,512]{1,0:T(8,128)(2,1)S(1)}, u32[]{:S(2)}, u32[]{:S(2)}) collective-permute-start(bf16[72,512]{1,0:T(8,128)(2,1)S(1)} %get-tuple-element.28.refs_3_), channel_id=1, source_target_pairs={{0,1},{1,0},{2,3},{3,2},{4,5},{5,4},{6,7},{7,6},{8,9},{9,8},{10,11... | collective-permute-start | bytes 221192 | tf_op jit(solution)/shard_map/ppermute | solution.py:184
  26.2 2.5 %collective-permute-start.10 = (bf16[72,512]{1,0:T(8,128)(2,1)S(1)}, bf16[72,512]{1,0:T(8,128)(2,1)S(1)}, u32[]{:S(2)}, u32[]{:S(2)}) collective-permute-start(bf16[72,512]{1,0:T(8,128)(2,1)S(1)} %collective-permute-done.7.refs_0_), channel_id=1, source_target_pairs={{0,1},{1,0},{2,3},{3,2},{4,5},{5,4},{6,7},{7,6},{8,9},{9,8},{10,11... | collective-permute-start | bytes 221192 | tf_op jit(solution)/shard_map/ppermute | solution.py:184
  27.6 1.3 %collective-permute-start.11 = (bf16[72,512]{1,0:T(8,128)(2,1)S(1)}, bf16[72,512]{1,0:T(8,128)(2,1)S(1)}, u32[]{:S(2)}, u32[]{:S(2)}) collective-permute-start(bf16[72,512]{1,0:T(8,128)(2,1)S(1)} %collective-permute-done.8.refs_1_), channel_id=1, source_target_pairs={{0,1},{1,0},{2,3},{3,2},{4,5},{5,4},{6,7},{7,6},{8,9},{9,8},{10,11... | collective-permute-start | bytes 221192 | tf_op jit(solution)/shard_map/ppermute | solution.py:184
  27.8 1.3 %collective-permute-start.12 = (bf16[72,512]{1,0:T(8,128)(2,1)S(1)}, bf16[72,512]{1,0:T(8,128)(2,1)S(1)}, u32[]{:S(2)}, u32[]{:S(2)}) collective-permute-start(bf16[72,512]{1,0:T(8,128)(2,1)S(1)} %collective-permute-done.9.refs_2_), channel_id=1, source_target_pairs={{0,1},{1,0},{2,3},{3,2},{4,5},{5,4},{6,7},{7,6},{8,9},{9,8},{10,11... | collective-permute-start | bytes 221192 | tf_op jit(solution)/shard_map/ppermute | solution.py:184

commit v2 on v1

--- a/solution.py
+++ b/solution.py
@@ -200,7 +200,7 @@
     columns = 2 * slots * width
 
     sibling = swap(trainer_panels, "tp", 1)
-    pairs = [(0, 0), *zip(range(1, groups - 1), range(groups - 2, 0, -1)), (groups - 1, groups - 1)]
+    pairs = [(0, 0), *zip(range(groups - 2, 0, -1), range(1, groups - 1)), (groups - 1, groups - 1)]
     if depth % 128 == 0:
         in_hbm = pltpu.with_memory_space_constraint(tokens, pltpu.HBM)
 

time: 30.5 us -> 30.6 us (level)
  no operation moved by 1% of the time
where the time goes in v2:
time: 30.6 us; the launch traced here: 30.4 us
  starting transfers between devices  14.6 us (48%)
  waiting for transfers between devices  9.03 us (30%)
  Pallas kernels  6.58 us (22%)
    ppermute x6, starting transfers between devices, swap_groups(): return lax.ppermute(x, ('grp', 'tp'), places)  9.63 us
    ppermute x8, waiting for transfers between devices, swap(): return lax.ppermute(x, axis, [(i, i ^ distance) for i in range(size)])  5.23 us
    ppermute x8, starting transfers between devices, swap(): return lax.ppermute(x, axis, [(i, i ^ distance) for i in range(size)])  5 us
    ppermute x6, waiting for transfers between devices, swap_groups(): return lax.ppermute(x, ('grp', 'tp'), places)  3.81 us
    pallas_call x3, Pallas kernels, cut(): call(functools.partial(split, turn, pairs), [jax.ShapeDtypeStruct((half,...  3.06 us
    pallas_call x3, Pallas kernels, products(): call(functools.partial(project, len(token_blocks)), [jax.ShapeDtypeStruct...  1.56 us
    pallas_call x1, Pallas kernels, on_device(): call(functools.partial(attend_rest, chips, steps), jax.ShapeDtypeStruct((...  1.26 us
  transfers between devices with their start and end apart: 14, of which 8 were waited for; matrix products, arithmetic and copies ran while one was open for 0% of the time, Pallas kernels for 17%

profile of v2, /device:TPU:0, one launch (start us, length us, event | category | flops | bytes accessed | tf_op | source)
XLA Modules:
  0.0 30.4 jit_solution(776031496295901775)
XLA Ops:
  0.0 0.5 %collective-permute-start = (bf16[4,1280,128]{2,1,0:T(8,128)(2,1)}, bf16[4,1280,128]{2,1,0:T(8,128)(2,1)S(1)}, u32[]{:S(2)}, u32[]{:S(2)}) collective-permute-start(bf16[4,1280,128]{2,1,0:T(8,128)(2,1)} %refs_2_.1), channel_id=1, source_target_pairs={{0,1},{1,0},{2,3},{3,2},{4,5},{5,4},{6,7},{7,6},{8,9},{9,8},{10,11... | collective-permute-start | bytes 3932168 | tf_op jit(solution)/shard_map/ppermute | solution.py:184
  0.5 1.0 %shard_map.46.refs_0_ = bf16[48,1280]{1,0:T(8,128)(2,1)S(1)} custom-call(bf16[96,5120]{1,0:T(8,128)(2,1)} %tokens.5), custom_call_target="tpu_custom_call" | custom-call | bytes 245760 | tf_op jit(solution)/shard_map/pallas_call | solution.py:209
  1.4 0.0 copy-start
  1.5 3.5 %collective-permute-start.1 = (bf16[48,1280]{1,0:T(8,128)(2,1)S(1)}, bf16[48,1280]{1,0:T(8,128)(2,1)S(1)}, u32[]{:S(2)}, u32[]{:S(2)}) collective-permute-start(bf16[48,1280]{1,0:T(8,128)(2,1)S(1)} %shard_map.46.refs_0_), channel_id=1, source_target_pairs={{0,24},{1,25},{2,26},{3,27},{4,28},{5,29},{6,30},{7,31},{8,16},{9,... | collective-permute-start | bytes 368648 | tf_op jit(solution)/shard_map/ppermute | solution.py:190
  5.0 1.1 %shard_map.47 = (bf16[48,1280]{1,0:T(8,128)(2,1)S(1)}, bf16[48,1280]{1,0:T(8,128)(2,1)S(1)}) custom-call(bf16[96,5120]{1,0:T(8,128)(2,1)} %tokens.5, bf16[48,1280]{1,0:T(8,128)(2,1)S(1)} %shard_map.46.refs_0_), custom_call_target="tpu_custom_call" | custom-call | bytes 491520 | tf_op jit(solution)/shard_map/pallas_call | solution.py:209
  6.1 0.6 %collective-permute-start.4 = (bf16[48,1280]{1,0:T(8,128)(2,1)S(1)}, bf16[48,1280]{1,0:T(8,128)(2,1)S(1)}, u32[]{:S(2)}, u32[]{:S(2)}) collective-permute-start(bf16[48,1280]{1,0:T(8,128)(2,1)S(1)} %get-tuple-element.22), channel_id=1, source_target_pairs={{0,8},{1,17},{2,10},{3,19},{4,12},{5,21},{6,14},{7,23},{8,0},{9,25... | collective-permute-start | bytes 368648 | tf_op jit(solution)/shard_map/ppermute | solution.py:190
  6.7 0.1 collective-permute-start.3
  6.8 1.0 %shard_map.48.refs_0_ = bf16[48,1280]{1,0:T(8,128)(2,1)S(1)} custom-call(bf16[96,5120]{1,0:T(8,128)(2,1)} %tokens.5, bf16[48,1280]{1,0:T(8,128)(2,1)S(1)} %get-tuple-element.19.refs_0_), custom_call_target="tpu_custom_call" | custom-call | bytes 245760 | tf_op jit(solution)/shard_map/pallas_call | solution.py:209
  7.8 0.0 collective-permute-done.refs_2_.refs_3_
  7.8 0.0 copy-done
  7.8 0.5 %shard_map.49.refs_0_ = f32[48,1024]{1,0:T(8,128)S(1)} custom-call(bf16[48,1280]{1,0:T(8,128)(2,1)S(1)} %shard_map.48.refs_0_, bf16[4,1280,128]{2,1,0:T(8,128)(2,1)S(1)} %copy-done, bf16[4,1280,128]{2,1,0:T(8,128)(2,1)S(1)} %collective-permute-done.refs_2_.refs_3_), custom_call_target="tpu_custom_call" | custom-call | flops 125829120 | bytes 2621440 | tf_op jit(solution)/shard_map/pallas_call | solution.py:234
  8.4 0.6 %collective-permute-done.1.refs_0_ = bf16[48,1280]{1,0:T(8,128)(2,1)S(1)} collective-permute-done((bf16[48,1280]{1,0:T(8,128)(2,1)S(1)}, bf16[48,1280]{1,0:T(8,128)(2,1)S(1)}, u32[]{:S(2)}, u32[]{:S(2)}) %collective-permute-start.1) | collective-permute-done | bytes 122912 | tf_op jit(solution)/shard_map/ppermute | solution.py:190
  9.0 0.5 %shard_map.50 = bf16[48,1024]{1,0:T(8,128)(2,1)S(1)} custom-call(bf16[48,1280]{1,0:T(8,128)(2,1)S(1)} %collective-permute-done.1.refs_0_, bf16[4,1280,128]{2,1,0:T(8,128)(2,1)S(1)} %copy-done, bf16[4,1280,128]{2,1,0:T(8,128)(2,1)S(1)} %collective-permute-done.refs_2_.refs_3_), custom_call_target="tpu_custom_call" | custom-call | flops 125829120 | bytes 2621440 | tf_op jit(solution)/shard_map/pallas_call | solution.py:234
  9.4 0.0 copy-start.1
  9.5 0.0 copy-start.2
  9.5 3.1 %collective-permute-start.2 = (bf16[48,1024]{1,0:T(8,128)(2,1)S(1)}, bf16[48,1024]{1,0:T(8,128)(2,1)S(1)}, u32[]{:S(2)}, u32[]{:S(2)}) collective-permute-start(bf16[48,1024]{1,0:T(8,128)(2,1)S(1)} %shard_map.50), channel_id=1, source_target_pairs={{0,24},{1,25},{2,26},{3,27},{4,28},{5,29},{6,30},{7,31},{8,16},{9,... | collective-permute-start | bytes 294920 | tf_op jit(solution)/shard_map/ppermute | solution.py:190
  12.6 0.0 collective-permute-done.4.refs_1_
  12.6 0.0 collective-permute-done.3.refs_0_
  12.6 0.6 %shard_map.51 = (bf16[48,1024]{1,0:T(8,128)(2,1)S(1)}, bf16[48,1024]{1,0:T(8,128)(2,1)S(1)}) custom-call(bf16[48,1280]{1,0:T(8,128)(2,1)S(1)} %collective-permute-done.3.refs_0_, bf16[48,1280]{1,0:T(8,128)(2,1)S(1)} %collective-permute-done.4.refs_1_, bf16[4,1280,128]{2,1,0:T(8,128)(2,1)S(1)} %copy-done, ...), custom_call_target="tpu_custom_call" | custom-call | flops 251658240 | bytes 2621440 | tf_op jit(solution)/shard_map/pallas_call | solution.py:234
  13.2 0.8 %collective-permute-start.5 = (bf16[48,1024]{1,0:T(8,128)(2,1)S(1)}, bf16[48,1024]{1,0:T(8,128)(2,1)S(1)}, u32[]{:S(2)}, u32[]{:S(2)}) collective-permute-start(bf16[48,1024]{1,0:T(8,128)(2,1)S(1)} %get-tuple-element.23), channel_id=1, source_target_pairs={{0,8},{1,17},{2,10},{3,19},{4,12},{5,21},{6,14},{7,23},{8,0},{9,25... | collective-permute-start | bytes 294920 | tf_op jit(solution)/shard_map/ppermute | solution.py:190
  14.0 1.4 %collective-permute-start.6 = (bf16[48,1024]{1,0:T(8,128)(2,1)S(1)}, bf16[48,1024]{1,0:T(8,128)(2,1)S(1)}, u32[]{:S(2)}, u32[]{:S(2)}) collective-permute-start(bf16[48,1024]{1,0:T(8,128)(2,1)S(1)} %get-tuple-element.24), channel_id=1, source_target_pairs={{0,16},{1,9},{2,18},{3,11},{4,20},{5,13},{6,22},{7,15},{8,24},{9,1... | collective-permute-start | bytes 294920 | tf_op jit(solution)/shard_map/ppermute | solution.py:190
  15.4 0.0 collective-permute-done.2.refs_1_
  15.4 3.0 %collective-permute-done.5.refs_2_ = bf16[48,1024]{1,0:T(8,128)(2,1)S(1)} collective-permute-done((bf16[48,1024]{1,0:T(8,128)(2,1)S(1)}, bf16[48,1024]{1,0:T(8,128)(2,1)S(1)}, u32[]{:S(2)}, u32[]{:S(2)}) %collective-permute-start.5) | collective-permute-done | bytes 98336 | tf_op jit(solution)/shard_map/ppermute | solution.py:190
  18.4 0.2 collective-permute-done.6.refs_3_
  18.6 0.1 shard_map.52
  18.7 2.6 %collective-permute-start.7 = (bf16[72,512]{1,0:T(8,128)(2,1)S(1)}, bf16[72,512]{1,0:T(8,128)(2,1)S(1)}, u32[]{:S(2)}, u32[]{:S(2)}) collective-permute-start(bf16[72,512]{1,0:T(8,128)(2,1)S(1)} %get-tuple-element.25), channel_id=1, source_target_pairs={{0,4},{1,5},{2,6},{3,7},{4,0},{5,1},{6,2},{7,3},{8,12},{9,13},{10,... | collective-permute-start | bytes 221192 | tf_op jit(solution)/shard_map/ppermute | solution.py:184
  21.4 1.3 %collective-permute-start.8 = (bf16[72,512]{1,0:T(8,128)(2,1)S(1)}, bf16[72,512]{1,0:T(8,128)(2,1)S(1)}, u32[]{:S(2)}, u32[]{:S(2)}) collective-permute-start(bf16[72,512]{1,0:T(8,128)(2,1)S(1)} %get-tuple-element.26), channel_id=1, source_target_pairs={{0,6},{1,7},{2,4},{3,5},{4,2},{5,3},{6,0},{7,1},{8,14},{9,15},{10,... | collective-permute-start | bytes 221192 | tf_op jit(solution)/shard_map/ppermute | solution.py:184
  22.7 0.2 collective-permute-start.9
  22.9 0.0 collective-permute-start.13
  22.9 3.1 %collective-permute-done.7.refs_0_ = bf16[72,512]{1,0:T(8,128)(2,1)S(1)} collective-permute-done((bf16[72,512]{1,0:T(8,128)(2,1)S(1)}, bf16[72,512]{1,0:T(8,128)(2,1)S(1)}, u32[]{:S(2)}, u32[]{:S(2)}) %collective-permute-start.7) | collective-permute-done | bytes 73760 | tf_op jit(solution)/shard_map/ppermute | solution.py:184
  26.1 0.0 collective-permute-start.10
  26.1 1.6 %collective-permute-done.8.refs_1_ = bf16[72,512]{1,0:T(8,128)(2,1)S(1)} collective-permute-done((bf16[72,512]{1,0:T(8,128)(2,1)S(1)}, bf16[72,512]{1,0:T(8,128)(2,1)S(1)}, u32[]{:S(2)}, u32[]{:S(2)}) %collective-permute-start.8) | collective-permute-done | bytes 73760 | tf_op jit(solution)/shard_map/ppermute | solution.py:184
  27.7 0.0 collective-permute-start.11
  27.7 0.2 collective-permute-done.9.refs_2_
  27.8 0.3 %collective-permute-start.12 = (bf16[72,512]{1,0:T(8,128)(2,1)S(1)}, bf16[72,512]{1,0:T(8,128)(2,1)S(1)}, u32[]{:S(2)}, u32[]{:S(2)}) collective-permute-start(bf16[72,512]{1,0:T(8,128)(2,1)S(1)} %collective-permute-done.9.refs_2_), channel_id=1, source_target_pairs={{0,1},{1,0},{2,3},{3,2},{4,5},{5,4},{6,7},{7,6},{8,9},{9,8},{10,11... | collective-permute-start | bytes 221192 | tf_op jit(solution)/shard_map/ppermute | solution.py:184
  28.2 0.0 copy-done.1
  28.2 0.0 copy-done.2
  28.2 0.6 %shard_map.53 = (bf16[128,128]{1,0:T(8,128)(2,1)S(1)}, f32[128,128]{1,0:T(8,128)S(1)}, f32[128,128]{1,0:T(8,128)S(1)}, f32[128,128]{1,0:T(8,128)S(1)}) custom-call(s32[1,24]{1,0:T(1,128)S(1)} %bitcast.1, s32[1,4]{1,0:T(1,128)S(1)} %copy-done.2, bf16[72,512]{1,0:T(8,128)(2,1)S(1)} %collective-permute-done.7.refs_0_, ...), custom_call_target="tpu_custom_call" | custom-call | bytes 393216 | tf_op jit(solution)/shard_map/pallas_call | solution.py:267
  28.8 0.0 collective-permute-done.13.refs_3_
  28.8 0.0 collective-permute-done.10.refs_0_
  28.8 0.1 collective-permute-done.11.refs_1_
  28.9 0.2 collective-permute-done.12.refs_2_
  29.1 1.3 %shard_map.54 = f32[12,1024]{1,0:T(8,128)} custom-call(s32[1,24]{1,0:T(1,128)S(1)} %bitcast.2, s32[1,4]{1,0:T(1,128)S(1)} %copy-done.2, bf16[128,128]{1,0:T(8,128)(2,1)S(1)} %get-tuple-element.29.queries, f32[128,128]{1,0:T(8,128)S(1)} %get-tuple-element.30.peak, f32[128,128]{1,0:T(8,128)S(1)} %get-tuple-element.31.mass, ...), custom_call_target="tpu_custom_call" | custom-call | bytes 393216 | tf_op jit(solution)/shard_map/pallas_call | solution.py:275
Async XLA Ops:
  0.0 7.8 %collective-permute-start = (bf16[4,1280,128]{2,1,0:T(8,128)(2,1)}, bf16[4,1280,128]{2,1,0:T(8,128)(2,1)S(1)}, u32[]{:S(2)}, u32[]{:S(2)}) collective-permute-start(bf16[4,1280,128]{2,1,0:T(8,128)(2,1)} %refs_2_.1), channel_id=1, source_target_pairs={{0,1},{1,0},{2,3},{3,2},{4,5},{5,4},{6,7},{7,6},{8,9},{9,8},{10,11... | collective-permute-start | bytes 3932168 | tf_op jit(solution)/shard_map/ppermute | solution.py:184
  1.4 6.4 %copy-start = (bf16[4,1280,128]{2,1,0:T(8,128)(2,1)S(1)}, bf16[4,1280,128]{2,1,0:T(8,128)(2,1)}, u32[]{:S(2)}) copy-start(bf16[4,1280,128]{2,1,0:T(8,128)(2,1)} %refs_2_.1) | copy-start | bytes 3932164
  1.5 7.5 %collective-permute-start.1 = (bf16[48,1280]{1,0:T(8,128)(2,1)S(1)}, bf16[48,1280]{1,0:T(8,128)(2,1)S(1)}, u32[]{:S(2)}, u32[]{:S(2)}) collective-permute-start(bf16[48,1280]{1,0:T(8,128)(2,1)S(1)} %shard_map.46.refs_0_), channel_id=1, source_target_pairs={{0,24},{1,25},{2,26},{3,27},{4,28},{5,29},{6,30},{7,31},{8,16},{9,... | collective-permute-start | bytes 368648 | tf_op jit(solution)/shard_map/ppermute | solution.py:190
  6.1 6.5 %collective-permute-start.4 = (bf16[48,1280]{1,0:T(8,128)(2,1)S(1)}, bf16[48,1280]{1,0:T(8,128)(2,1)S(1)}, u32[]{:S(2)}, u32[]{:S(2)}) collective-permute-start(bf16[48,1280]{1,0:T(8,128)(2,1)S(1)} %get-tuple-element.22), channel_id=1, source_target_pairs={{0,8},{1,17},{2,10},{3,19},{4,12},{5,21},{6,14},{7,23},{8,0},{9,25... | collective-permute-start | bytes 368648 | tf_op jit(solution)/shard_map/ppermute | solution.py:190
  6.7 5.9 %collective-permute-start.3 = (bf16[48,1280]{1,0:T(8,128)(2,1)S(1)}, bf16[48,1280]{1,0:T(8,128)(2,1)S(1)}, u32[]{:S(2)}, u32[]{:S(2)}) collective-permute-start(bf16[48,1280]{1,0:T(8,128)(2,1)S(1)} %get-tuple-element.19.refs_0_), channel_id=1, source_target_pairs={{0,16},{1,9},{2,18},{3,11},{4,20},{5,13},{6,22},{7,15},{8,24},{9,1... | collective-permute-start | bytes 368648 | tf_op jit(solution)/shard_map/ppermute | solution.py:190
  9.4 18.7 %copy-start.1 = (s32[24]{0:T(128)S(1)}, s32[24]{0:T(128)}, u32[]{:S(2)}) copy-start(s32[24]{0:T(128)} %param.6) | copy-start | bytes 292
  9.5 18.7 %copy-start.2 = (s32[1,4]{1,0:T(1,128)S(1)}, s32[1,4]{1,0:T(1,128)}, u32[]{:S(2)}) copy-start(s32[1,4]{1,0:T(1,128)} %lengths.3) | copy-start | bytes 52
  9.5 5.9 %collective-permute-start.2 = (bf16[48,1024]{1,0:T(8,128)(2,1)S(1)}, bf16[48,1024]{1,0:T(8,128)(2,1)S(1)}, u32[]{:S(2)}, u32[]{:S(2)}) collective-permute-start(bf16[48,1024]{1,0:T(8,128)(2,1)S(1)} %shard_map.50), channel_id=1, source_target_pairs={{0,24},{1,25},{2,26},{3,27},{4,28},{5,29},{6,30},{7,31},{8,16},{9,... | collective-permute-start | bytes 294920 | tf_op jit(solution)/shard_map/ppermute | solution.py:190
  13.2 5.2 %collective-permute-start.5 = (bf16[48,1024]{1,0:T(8,128)(2,1)S(1)}, bf16[48,1024]{1,0:T(8,128)(2,1)S(1)}, u32[]{:S(2)}, u32[]{:S(2)}) collective-permute-start(bf16[48,1024]{1,0:T(8,128)(2,1)S(1)} %get-tuple-element.23), channel_id=1, source_target_pairs={{0,8},{1,17},{2,10},{3,19},{4,12},{5,21},{6,14},{7,23},{8,0},{9,25... | collective-permute-start | bytes 294920 | tf_op jit(solution)/shard_map/ppermute | solution.py:190
  14.0 4.6 %collective-permute-start.6 = (bf16[48,1024]{1,0:T(8,128)(2,1)S(1)}, bf16[48,1024]{1,0:T(8,128)(2,1)S(1)}, u32[]{:S(2)}, u32[]{:S(2)}) collective-permute-start(bf16[48,1024]{1,0:T(8,128)(2,1)S(1)} %get-tuple-element.24), channel_id=1, source_target_pairs={{0,16},{1,9},{2,18},{3,11},{4,20},{5,13},{6,22},{7,15},{8,24},{9,1... | collective-permute-start | bytes 294920 | tf_op jit(solution)/shard_map/ppermute | solution.py:190
  18.7 7.3 %collective-permute-start.7 = (bf16[72,512]{1,0:T(8,128)(2,1)S(1)}, bf16[72,512]{1,0:T(8,128)(2,1)S(1)}, u32[]{:S(2)}, u32[]{:S(2)}) collective-permute-start(bf16[72,512]{1,0:T(8,128)(2,1)S(1)} %get-tuple-element.25), channel_id=1, source_target_pairs={{0,4},{1,5},{2,6},{3,7},{4,0},{5,1},{6,2},{7,3},{8,12},{9,13},{10,... | collective-permute-start | bytes 221192 | tf_op jit(solution)/shard_map/ppermute | solution.py:184
  21.4 6.3 %collective-permute-start.8 = (bf16[72,512]{1,0:T(8,128)(2,1)S(1)}, bf16[72,512]{1,0:T(8,128)(2,1)S(1)}, u32[]{:S(2)}, u32[]{:S(2)}) collective-permute-start(bf16[72,512]{1,0:T(8,128)(2,1)S(1)} %get-tuple-element.26), channel_id=1, source_target_pairs={{0,6},{1,7},{2,4},{3,5},{4,2},{5,3},{6,0},{7,1},{8,14},{9,15},{10,... | collective-permute-start | bytes 221192 | tf_op jit(solution)/shard_map/ppermute | solution.py:184
  22.7 5.1 %collective-permute-start.9 = (bf16[72,512]{1,0:T(8,128)(2,1)S(1)}, bf16[72,512]{1,0:T(8,128)(2,1)S(1)}, u32[]{:S(2)}, u32[]{:S(2)}) collective-permute-start(bf16[72,512]{1,0:T(8,128)(2,1)S(1)} %get-tuple-element.27), channel_id=1, source_target_pairs={{0,2},{1,3},{2,0},{3,1},{4,6},{5,7},{6,4},{7,5},{8,10},{9,11},{10,... | collective-permute-start | bytes 221192 | tf_op jit(solution)/shard_map/ppermute | solution.py:184
  22.9 5.8 %collective-permute-start.13 = (bf16[72,512]{1,0:T(8,128)(2,1)S(1)}, bf16[72,512]{1,0:T(8,128)(2,1)S(1)}, u32[]{:S(2)}, u32[]{:S(2)}) collective-permute-start(bf16[72,512]{1,0:T(8,128)(2,1)S(1)} %get-tuple-element.28.refs_3_), channel_id=1, source_target_pairs={{0,1},{1,0},{2,3},{3,2},{4,5},{5,4},{6,7},{7,6},{8,9},{9,8},{10,11... | collective-permute-start | bytes 221192 | tf_op jit(solution)/shard_map/ppermute | solution.py:184
  26.1 2.7 %collective-permute-start.10 = (bf16[72,512]{1,0:T(8,128)(2,1)S(1)}, bf16[72,512]{1,0:T(8,128)(2,1)S(1)}, u32[]{:S(2)}, u32[]{:S(2)}) collective-permute-start(bf16[72,512]{1,0:T(8,128)(2,1)S(1)} %collective-permute-done.7.refs_0_), channel_id=1, source_target_pairs={{0,1},{1,0},{2,3},{3,2},{4,5},{5,4},{6,7},{7,6},{8,9},{9,8},{10,11... | collective-permute-start | bytes 221192 | tf_op jit(solution)/shard_map/ppermute | solution.py:184
  27.7 1.3 %collective-permute-start.11 = (bf16[72,512]{1,0:T(8,128)(2,1)S(1)}, bf16[72,512]{1,0:T(8,128)(2,1)S(1)}, u32[]{:S(2)}, u32[]{:S(2)}) collective-permute-start(bf16[72,512]{1,0:T(8,128)(2,1)S(1)} %collective-permute-done.8.refs_1_), channel_id=1, source_target_pairs={{0,1},{1,0},{2,3},{3,2},{4,5},{5,4},{6,7},{7,6},{8,9},{9,8},{10,11... | collective-permute-start | bytes 221192 | tf_op jit(solution)/shard_map/ppermute | solution.py:184
  27.8 1.3 %collective-permute-start.12 = (bf16[72,512]{1,0:T(8,128)(2,1)S(1)}, bf16[72,512]{1,0:T(8,128)(2,1)S(1)}, u32[]{:S(2)}, u32[]{:S(2)}) collective-permute-start(bf16[72,512]{1,0:T(8,128)(2,1)S(1)} %collective-permute-done.9.refs_2_), channel_id=1, source_target_pairs={{0,1},{1,0},{2,3},{3,2},{4,5},{5,4},{6,7},{7,6},{8,9},{9,8},{10,11... | collective-permute-start | bytes 221192 | tf_op jit(solution)/shard_map/ppermute | solution.py:184
